TPU v7x, 32 devices: a whole 2x2x4 slice. The times are simulated.
32 devices in a mesh: groups: 2 (over y), dp: 4 (over z), ctx: 4 (over x, core).
Axes of the slice: x: 2, y: 2, z: 4, core: 2. Of those that a mesh axis runs over, the one named last changes fastest.
Arguments:
- queries: bfloat16 [8, 1024, 2048], P(('groups', 'dp'), 'ctx'), parts along dimension 0, may hold values from -480 to 480
- keys: bfloat16 [8, 1024, 256], P(('groups', 'dp'), 'ctx'), parts along dimension 0, may hold values from -4.1 to 4.1
- values: bfloat16 [8, 1024, 256], P(('groups', 'dp'), 'ctx'), parts along dimension 0, may hold values from -6 to 6
- grad_out: bfloat16 [8, 1024, 2048], P(('groups', 'dp'), 'ctx'), parts along dimension 0, may hold values from -6 to 6
- sinks: float32 [32], replicated, may hold values from 0 to 6
- doc_ids: int32 [8, 1024], P(('groups', 'dp')), parts along dimension 0, may hold values from 0 to 1, never falling along the last dimension, each value on 1 to 768 neighbouring positions
- swap_flags: int32 [8, 4, 16], P(('groups', 'dp'), 'ctx'), parts along dimension 0, may hold values from 0 to 1, as said below
Outputs:
- attn_out: bfloat16 [8, 1024, 2048], P(('groups', 'dp'), 'ctx'), parts along dimension 0
- grad_queries: bfloat16 [8, 1024, 2048], P(('groups', 'dp'), 'ctx'), parts along dimension 0
- grad_keys: bfloat16 [8, 1024, 256], P(('groups', 'dp'), 'ctx'), parts along dimension 0
- grad_values: bfloat16 [8, 1024, 256], P(('groups', 'dp'), 'ctx'), parts along dimension 0
There are 2 independent parts, one for each index of `groups`. A program takes and returns all parts, laid end to end along the dimension named above; an argument that names none is the same for every part. Nothing has to cross between parts.
Inputs may be any that keep to these rules, and one draw needn't show every extreme that they name: `doc_ids`: each of the 2 responses of a pack covers between 256 and 768 neighbouring positions. swap_flags of rank i and run c equal those of its partner rank (i + 2) mod 4 and run c; each device has at most 1 ones, and some device has exactly 1.
All inputs are finite; a program needn't handle non-finite values.
Results may differ from a plain program's by a relative error of at most 0.019.
Values may be sent and summed in bfloat16 or wider, within the bound.
A program may use at most 64 MiB of HBM per device.

v0:
```python
import math

import jax
import jax.numpy as jnp
from jax import lax
from jax.sharding import PartitionSpec as P

QUERY_HEADS = 32
KEY_VALUE_HEADS = 4
HEAD_SIZE = 64
WINDOW = 128
CAP = 1


def swapped(block, axis, apart):
    count = lax.axis_size(axis)
    route = []
    for low in range(count):
        high = low | 1 << apart
        if high != low and high < count:
            route += [(low, high), (high, low)]
    return lax.ppermute(block, axis, route)


def shifted(value, axis, steps):
    count = lax.axis_size(axis)
    initial, last = (max(0, -steps), min(count, count - steps))
    return lax.ppermute(value, axis, [(source, source + steps) for source in range(initial, last)])


def reach_partner(outgoing):
    return swapped(outgoing, "dp", lax.axis_size("dp").bit_length() - 2)


def shards(queries, keys, values, grad_out, sinks, doc_ids, swap_flags):
    row_count = queries.shape[1]
    swap_marks = swap_flags[0, 0]
    block_count = swap_marks.shape[0]
    block_rows = row_count // block_count
    query_width = queries.shape[2]
    key_span_width = keys.shape[2]
    heads_per_group = QUERY_HEADS // KEY_VALUE_HEADS
    group_width = heads_per_group * HEAD_SIZE
    score_scale = 1.0 / math.sqrt(HEAD_SIZE)
    filled = jnp.cumsum(swap_marks) - 1
    slot_numbers = jnp.arange(CAP, dtype=jnp.int32)
    block_numbers = jnp.arange(block_count, dtype=jnp.int32)
    hits = (swap_marks[None, :] == 1) & (filled[None, :] == slot_numbers[:, None])
    chosen = jnp.sum(jnp.where(hits, block_numbers[None, :], 0), axis=1)
    landing = jnp.clip(filled, 0, CAP - 1)

    def trade(rows_data):
        width = rows_data.shape[1]
        blocked = rows_data.reshape(block_count, block_rows, width)
        outgoing = jnp.take(blocked, chosen, axis=0)
        incoming = reach_partner(outgoing)
        spread = jnp.take(incoming, landing, axis=0)
        return jnp.where(swap_marks[:, None, None] == 1, spread, blocked).reshape(row_count, width)

    bundle = trade(jnp.concatenate([queries[0], keys[0], values[0], grad_out[0]], axis=1))
    pack_q = bundle[:, :query_width]
    pack_k = bundle[:, query_width : query_width + key_span_width]
    pack_v = bundle[:, query_width + key_span_width : query_width + 2 * key_span_width]
    pack_g = bundle[:, query_width + 2 * key_span_width :]
    tail_rows = jnp.concatenate([pack_k, pack_v], axis=1)[row_count - WINDOW :]
    halo_rows = shifted(tail_rows, "ctx", 1)
    key_all = jnp.concatenate([halo_rows[:, :key_span_width], pack_k], axis=0)
    value_all = jnp.concatenate([halo_rows[:, key_span_width:], pack_v], axis=0)
    span = row_count + WINDOW
    offset = lax.axis_index("ctx") * row_count
    pack_docs = doc_ids[0]
    docs_pad = jnp.concatenate([jnp.full((WINDOW,), -1, jnp.int32), pack_docs], axis=0)
    query_docs = lax.dynamic_slice_in_dim(pack_docs, offset, row_count, 0)
    key_docs = lax.dynamic_slice_in_dim(docs_pad, offset, span, 0)
    distance = (
        jnp.arange(row_count, dtype=jnp.int32)[:, None]
        + WINDOW
        - jnp.arange(span, dtype=jnp.int32)[None, :]
    )
    allowed = (query_docs[:, None] == key_docs[None, :]) & (distance >= 0) & (distance < WINDOW)
    saved = []
    out_parts = []
    for key_value_group in range(KEY_VALUE_HEADS):
        query_group = pack_q[
            :, key_value_group * group_width : (key_value_group + 1) * group_width
        ].reshape(row_count, heads_per_group, HEAD_SIZE)
        key_group = key_all[:, key_value_group * HEAD_SIZE : (key_value_group + 1) * HEAD_SIZE]
        value_group = value_all[:, key_value_group * HEAD_SIZE : (key_value_group + 1) * HEAD_SIZE]
        sink_group = sinks[
            key_value_group * heads_per_group : (key_value_group + 1) * heads_per_group
        ][:, None]
        scores = (
            jnp.einsum("rgd,ld->grl", query_group, key_group, preferred_element_type=jnp.float32)
            * score_scale
        )
        masked = jnp.where(allowed, scores, jnp.float32(-1e30))
        top = jnp.maximum(jnp.max(masked, axis=-1), sink_group)
        expo = jnp.where(allowed, jnp.exp(masked - top[..., None]), jnp.float32(0.0))
        total = jnp.exp(sink_group - top) + jnp.sum(expo, axis=-1)
        probs = expo / total[..., None]
        probs_b = probs.astype(jnp.bfloat16)
        out_group = jnp.einsum(
            "grl,ld->rgd", probs_b, value_group, preferred_element_type=jnp.float32
        ).astype(jnp.bfloat16)
        saved.append((probs, probs_b, out_group))
        out_parts.append(out_group.reshape(row_count, group_width))
    pack_out = jnp.concatenate(out_parts, axis=1)
    final_out = trade(pack_out)
    dq_parts = []
    dk_parts = []
    dv_parts = []
    for key_value_group in range(KEY_VALUE_HEADS):
        probs, probs_b, out_group = saved[key_value_group]
        query_group = pack_q[
            :, key_value_group * group_width : (key_value_group + 1) * group_width
        ].reshape(row_count, heads_per_group, HEAD_SIZE)
        grad_group = pack_g[
            :, key_value_group * group_width : (key_value_group + 1) * group_width
        ].reshape(row_count, heads_per_group, HEAD_SIZE)
        key_group = key_all[:, key_value_group * HEAD_SIZE : (key_value_group + 1) * HEAD_SIZE]
        value_group = value_all[:, key_value_group * HEAD_SIZE : (key_value_group + 1) * HEAD_SIZE]
        row_dot = jnp.einsum(
            "rgd,rgd->gr", grad_group.astype(jnp.float32), out_group.astype(jnp.float32)
        )
        dprobs = jnp.einsum(
            "rgd,ld->grl", grad_group, value_group, preferred_element_type=jnp.float32
        )
        dscores_b = (probs * (dprobs - row_dot[..., None])).astype(jnp.bfloat16)
        query_gradient = (
            jnp.einsum("grl,ld->rgd", dscores_b, key_group, preferred_element_type=jnp.float32)
            * score_scale
        )
        dq_parts.append(query_gradient.astype(jnp.bfloat16).reshape(row_count, group_width))
        dk_parts.append(
            jnp.einsum("grl,rgd->ld", dscores_b, query_group, preferred_element_type=jnp.float32)
            * score_scale
        )
        dv_parts.append(
            jnp.einsum("grl,rgd->ld", probs_b, grad_group, preferred_element_type=jnp.float32)
        )
    pack_dq = jnp.concatenate(dq_parts, axis=1)
    grad_k_all = jnp.concatenate(dk_parts, axis=1)
    grad_v_all = jnp.concatenate(dv_parts, axis=1)
    returned = shifted(
        jnp.concatenate([grad_k_all[:WINDOW], grad_v_all[:WINDOW]], axis=1), "ctx", -1
    )
    grad_k_own = grad_k_all[WINDOW:].at[row_count - WINDOW :].add(returned[:, :key_span_width])
    grad_v_own = grad_v_all[WINDOW:].at[row_count - WINDOW :].add(returned[:, key_span_width:])
    pack_dk = grad_k_own.astype(jnp.bfloat16)
    pack_dv = grad_v_own.astype(jnp.bfloat16)
    gradients = trade(jnp.concatenate([pack_dq, pack_dk, pack_dv], axis=1))
    final_dq = gradients[:, :query_width]
    final_dk = gradients[:, query_width : query_width + key_span_width]
    final_dv = gradients[:, query_width + key_span_width :]
    return (final_out[None], final_dq[None], final_dk[None], final_dv[None])


def solution(mesh):
    in_specs = (
        P(("groups", "dp"), "ctx", None),
        P(("groups", "dp"), "ctx", None),
        P(("groups", "dp"), "ctx", None),
        P(("groups", "dp"), "ctx", None),
        P(),
        P(("groups", "dp"), None),
        P(("groups", "dp"), "ctx", None),
    )
    out_specs = (
        P(("groups", "dp"), "ctx", None),
        P(("groups", "dp"), "ctx", None),
        P(("groups", "dp"), "ctx", None),
        P(("groups", "dp"), "ctx", None),
    )
    return jax.shard_map(shards, mesh=mesh, in_specs=in_specs, out_specs=out_specs, check_vma=False)
```

profile of v0, /device:TPU:11, one launch (start us, length us, event | category | flops | bytes accessed | tf_op | source)
XLA Modules:
  0.0 97.5 jit_solution(12434777906133009077)
XLA Ops:
  1.7 1.3 %fusion.84 = s32[]{:T(128)} fusion(pred[16]{0:T(512)(128)(4,1)S(1)} %get-tuple-element.69, s32[1,1,16]{2,1,0:T(1,128)} %param.17), kind=kLoop, calls=%fused_computation.169 | loop fusion | flops 63 | bytes 84 | tf_op jit(solution)/shard_map/reduce_sum | solution.py:49
  5.0 1.6 %broadcast_select_fusion = bf16[1,16,4608]{2,1,0:T(8,128)(2,1)} fusion(pred[]{:T(512)} %bitcast.12, s32[]{:T(128)} %bitcast.17, bf16[16,16,2048]{2,1,0:T(8,128)(2,1)} %bitcast.285, bf16[16,16,256]{2,1,0:T(8,128)(2,1)} %bitcast.316, bf16[16,16,256]{2,1,0:T(8,128)(2,1)} %bitcast.315, bf16[16,16,2048]{2,1,0:T(8,128)(2,1)} %bitcast.284), kind=kLoop, calls=%fused_computation.109 | loop fusion | flops 663552 | bytes 2506757 | tf_op jit(solution)/shard_map/jit(_take)/select_n | solution.py:55
  6.6 2.3 %collective-permute-start = (bf16[1,16,4608]{2,1,0:T(8,128)(2,1)}, bf16[1,16,4608]{2,1,0:T(8,128)(2,1)S(1)}, u32[]{:S(2)}, u32[]{:S(2)}) collective-permute-start(bf16[1,16,4608]{2,1,0:T(8,128)(2,1)} %broadcast_select_fusion), channel_id=1, source_target_pairs={{0,8},{8,0},{4,12},{12,4},{1,9},{9,1},{5,13},{13,5},{2,10},{10,2},... | collective-permute-start | bytes 442376 | tf_op jit(solution)/shard_map/ppermute | solution.py:22
  9.5 1.7 %copy.48 = bf16[1,256,256]{1,2,0:T(8,128)(2,1)} copy(bf16[1,256,256]{2,1,0:T(8,128)(2,1)} %param.12) | data formatting | bytes 262144 | tf_op args[1]
  11.2 1.7 %copy.49 = bf16[1,256,256]{1,2,0:T(8,128)(2,1)} copy(bf16[1,256,256]{2,1,0:T(8,128)(2,1)} %param.13) | data formatting | bytes 262144 | tf_op args[2]
  13.4 1.3 %copy.50 = bf16[1,256,2048]{1,2,0:T(8,128)(2,1)} copy(bf16[1,256,2048]{2,1,0:T(8,128)(2,1)S(1)} %copy-done.1) | data formatting | bytes 2097152 | tf_op args[3]
  16.5 1.1 %broadcast.422 = bf16[16,16,4608]{2,1,0:T(8,128)(2,1)S(1)} broadcast(bf16[16,4608]{1,0:T(8,128)(2,1)} %bitcast.327), dimensions={1,2} | broadcast | bytes 2506752 | tf_op jit(solution)/shard_map/jit(_take)/gather | solution.py:57
  17.6 2.4 %copy.46 = bf16[256,4608]{0,1:T(8,128)(2,1)} copy(bf16[256,4608]{1,0:T(8,128)(2,1)S(1)} %bitcast.283) | data formatting | bytes 4718592 | tf_op jit(solution)/shard_map/jit(_take)/gather | solution.py:57
  20.0 2.4 %maximum_select_fusion = bf16[256,4608]{0,1:T(8,128)(2,1)S(1)} fusion(bf16[256,2048]{0,1:T(8,128)(2,1)} %bitcast.288, bf16[256,256]{0,1:T(8,128)(2,1)} %bitcast.318, bf16[256,256]{0,1:T(8,128)(2,1)} %bitcast.317, bf16[256,2048]{0,1:T(8,128)(2,1)S(1)} %bitcast.287, bf16[256,4608]{0,1:T(8,128)(2,1)} %copy.46, pred[256]{0:T(512)(128)(4,1)S(1)} %broadcast_in_dim.156, ...), kind=kLoop, calls=%fused_computation.24 | loop fusion | flops 11796480 | bytes 7078400 | tf_op jit(solution)/shard_map/jit(_where)/select_n | solution.py:58
  22.6 1.3 %collective-permute-start.1 = (bf16[128,512]{0,1:T(8,128)(2,1)S(1)}, bf16[128,512]{0,1:T(8,128)(2,1)S(1)}, u32[]{:S(2)}, u32[]{:S(2)}) collective-permute-start(bf16[128,512]{0,1:T(8,128)(2,1)S(1)} %slice.229), channel_id=1, source_target_pairs={{0,1},{1,2},{2,3},{4,5},{5,6},{6,7},{8,9},{9,10},{10,11},{12,13},{... | collective-permute-start | bytes 393224 | tf_op jit(solution)/shard_map/ppermute | solution.py:28
  23.9 1.9 %collective-permute-done.1 = bf16[128,512]{0,1:T(8,128)(2,1)S(1)} collective-permute-done((bf16[128,512]{0,1:T(8,128)(2,1)S(1)}, bf16[128,512]{0,1:T(8,128)(2,1)S(1)}, u32[]{:S(2)}, u32[]{:S(2)}) %collective-permute-start.1) | collective-permute-done | bytes 131104 | tf_op jit(solution)/shard_map/ppermute | solution.py:28
  27.8 2.3 %fusion.13 = (f32[8,256]{1,0:T(8,128)S(1)}, f32[8,256]{1,0:T(8,128)S(1)}, f32[8,256]{1,0:T(8,128)S(1)}, f32[8,256]{1,0:T(8,128)S(1)}, f32[384,256,8]{1,0,2:T(8,128)S(1)}) fusion(f32[384,256,8]{1,0,2:T(8,128)S(1)} %get-tuple-element.101, f32[8,256]{1,0:T(8,128)S(1)} %broadcast_maximum_fusion.3, pred[256,384]{0,1:T(8,128)(4,1)S(1)} %fusion.44, ...), kind=kOutput, calls=%fused_computation.30 | convolution fusion | flops 111763456 | bytes 13180928 | tf_op jit(solution)/shard_map/rgd,ld->grl/dot_general | solution.py:93
  30.4 2.4 %fusion.15 = (f32[8,256]{1,0:T(8,128)S(1)}, f32[8,256]{1,0:T(8,128)S(1)}, f32[8,256]{1,0:T(8,128)S(1)}) fusion(f32[384,256,8]{1,0,2:T(8,128)S(1)} %get-tuple-element.102, f32[8,256]{1,0:T(8,128)S(1)} %broadcast_maximum_fusion.2, pred[256,384]{0,1:T(8,128)(4,1)S(1)} %fusion.44, f32[8,256]{1,0:T(8,128)S(1)} %broadcast_maximum_fusion.1, ...), kind=kLoop, calls=%fused_computation.32 | loop fusion | flops 11790336 | bytes 9584640 | tf_op jit(solution)/shard_map/reduce_sum | solution.py:99
  33.0 1.1 %convolution_convert_fusion.1 = bf16[64,8,256]{2,0,1:T(8,128)(2,1)S(1)} fusion(bf16[256,256]{0,1:T(8,128)(2,1)S(1)} %get-tuple-element.89, bf16[128,256]{0,1:T(8,128)(2,1)S(1)} %get-tuple-element.95, f32[384,256,8]{1,0,2:T(8,128)S(1)} %fusion.81, f32[8,256]{1,0:T(8,128)S(1)} %exponential_add_fusion.1, f32[8,256]{1,0:T(8,128)S(1)} %broadcast_maximum_fusion.1, ...), kind=kOutput, calls=%fused_computation.48 | convolution fusion | flops 105611264 | bytes 3719168 | tf_op jit(solution)/shard_map/grl,ld->rgd/dot_general | solution.py:102
  34.1 1.1 %convolution_convert_fusion.2 = bf16[64,8,256]{2,0,1:T(8,128)(2,1)S(1)} fusion(bf16[256,256]{0,1:T(8,128)(2,1)S(1)} %get-tuple-element.89, bf16[128,256]{0,1:T(8,128)(2,1)S(1)} %get-tuple-element.95, f32[384,256,8]{1,0,2:T(8,128)S(1)} %get-tuple-element.102, f32[8,256]{1,0:T(8,128)S(1)} %exponential_add_fusion.2, f32[8,256]{1,0:T(8,128)S(1)} %broadcast_maximum_fusion.2, ...), kind=kOutput, calls=%fused_computation.49 | convolution fusion | flops 105611264 | bytes 3719168 | tf_op jit(solution)/shard_map/grl,ld->rgd/dot_general | solution.py:102
  35.2 1.1 %convolution_convert_fusion.3 = bf16[64,8,256]{2,0,1:T(8,128)(2,1)S(1)} fusion(bf16[256,256]{0,1:T(8,128)(2,1)S(1)} %get-tuple-element.89, bf16[128,256]{0,1:T(8,128)(2,1)S(1)} %get-tuple-element.95, f32[384,256,8]{1,0,2:T(8,128)S(1)} %get-tuple-element.101, f32[8,256]{1,0:T(8,128)S(1)} %exponential_add_fusion.3, f32[8,256]{1,0:T(8,128)S(1)} %broadcast_maximum_fusion.3, ...), kind=kOutput, calls=%fused_computation.50 | convolution fusion | flops 105611264 | bytes 3719168 | tf_op jit(solution)/shard_map/grl,ld->rgd/dot_general | solution.py:102
  36.3 1.1 %convolution_convert_fusion = bf16[64,8,256]{2,0,1:T(8,128)(2,1)S(1)} fusion(bf16[384,64,1]{0,1,2:T(8,128)(2,1)S(1)} %get-tuple-element.104, f32[384,256,8]{1,0,2:T(8,128)S(1)} %fusion.109, f32[8,256]{1,0:T(8,128)S(1)} %exponential_add_fusion, f32[8,256]{1,0:T(8,128)S(1)} %broadcast_maximum_fusion, pred[256,384]{0,1:T(8,128)(4,1)S(1)} %fusion.44), kind=kOutput, calls=%fused_computation.47 | convolution fusion | flops 105512960 | bytes 3571712 | tf_op jit(solution)/shard_map/grl,ld->rgd/dot_general | solution.py:102
  37.9 1.1 %convolution_bitcast_fusion = f32[384,64]{0,1:T(8,128)S(1)} fusion(bf16[256,8,64]{0,2,1:T(8,128)(2,1)S(1)} %bitcast.325, f32[384,256,8]{1,0,2:T(8,128)S(1)} %fusion.109, f32[8,256]{1,0:T(8,128)S(1)} %exponential_add_fusion, f32[8,256]{1,0:T(8,128)S(1)} %broadcast_maximum_fusion, pred[256,384]{0,1:T(8,128)(4,1)S(1)} %fusion.44), kind=kOutput, calls=%fused_computation.51 | convolution fusion | flops 105381888 | bytes 3620864 | tf_op jit(solution)/shard_map/grl,rgd->ld/dot_general | solution.py:139
  39.0 1.2 %fusion.1 = bf16[8,256,384]{1,2,0:T(8,128)(2,1)S(1)} fusion(bf16[384,64,1]{0,1,2:T(8,128)(2,1)S(1)} %get-tuple-element.104, bf16[256,8,64]{0,2,1:T(8,128)(2,1)S(1)} %bitcast.326, f32[8,256]{1,0:T(8,128)S(1)} %get-tuple-element.70, f32[8,256]{1,0:T(8,128)S(1)} %exponential_add_fusion, f32[8,256]{1,0:T(8,128)S(1)} %broadcast_maximum_fusion, ...), kind=kOutput, calls=%fused_computation.2 | convolution fusion | flops 106954752 | bytes 5152768 | tf_op jit(solution)/shard_map/rgd,ld->grl/dot_general | solution.py:125
  41.2 1.1 %convolution_bitcast_fusion.1 = f32[384,64]{0,1:T(8,128)S(1)} fusion(bf16[256,8,64]{0,2,1:T(8,128)(2,1)S(1)} %bitcast.323, f32[384,256,8]{1,0,2:T(8,128)S(1)} %fusion.81, f32[8,256]{1,0:T(8,128)S(1)} %exponential_add_fusion.1, f32[8,256]{1,0:T(8,128)S(1)} %broadcast_maximum_fusion.1, pred[256,384]{0,1:T(8,128)(4,1)S(1)} %fusion.44), kind=kOutput, calls=%fused_computation.52 | convolution fusion | flops 105381888 | bytes 3620864 | tf_op jit(solution)/shard_map/grl,rgd->ld/dot_general | solution.py:139
  42.3 1.2 %fusion.3 = bf16[8,256,384]{1,2,0:T(8,128)(2,1)S(1)} fusion(bf16[256,8,64]{0,2,1:T(8,128)(2,1)S(1)} %bitcast.324, f32[8,256]{1,0:T(8,128)S(1)} %get-tuple-element.78, bf16[256,256]{0,1:T(8,128)(2,1)S(1)} %get-tuple-element.89, bf16[128,256]{0,1:T(8,128)(2,1)S(1)} %get-tuple-element.95, f32[8,256]{1,0:T(8,128)S(1)} %exponential_add_fusion.1, ...), kind=kOutput, calls=%fused_computation.5 | convolution fusion | flops 107053056 | bytes 5300224 | tf_op jit(solution)/shard_map/rgd,ld->grl/dot_general | solution.py:125
  44.5 1.1 %convolution_bitcast_fusion.2 = f32[384,64]{0,1:T(8,128)S(1)} fusion(bf16[256,8,64]{0,2,1:T(8,128)(2,1)S(1)} %bitcast.321, f32[384,256,8]{1,0,2:T(8,128)S(1)} %get-tuple-element.102, f32[8,256]{1,0:T(8,128)S(1)} %exponential_add_fusion.2, f32[8,256]{1,0:T(8,128)S(1)} %broadcast_maximum_fusion.2, pred[256,384]{0,1:T(8,128)(4,1)S(1)} %fusion.44), kind=kOutput, calls=%fused_computation.53 | convolution fusion | flops 105381888 | bytes 3620864 | tf_op jit(solution)/shard_map/grl,rgd->ld/dot_general | solution.py:139
  45.6 1.2 %fusion.5 = bf16[8,256,384]{1,2,0:T(8,128)(2,1)S(1)} fusion(bf16[256,8,64]{0,2,1:T(8,128)(2,1)S(1)} %bitcast.322, f32[8,256]{1,0:T(8,128)S(1)} %get-tuple-element.80, bf16[256,256]{0,1:T(8,128)(2,1)S(1)} %get-tuple-element.89, bf16[128,256]{0,1:T(8,128)(2,1)S(1)} %get-tuple-element.95, f32[8,256]{1,0:T(8,128)S(1)} %exponential_add_fusion.2, ...), kind=kOutput, calls=%fused_computation.8 | convolution fusion | flops 107053056 | bytes 5300224 | tf_op jit(solution)/shard_map/rgd,ld->grl/dot_general | solution.py:125
  48.0 1.1 %convolution_bitcast_fusion.3 = f32[384,64]{0,1:T(8,128)S(1)} fusion(bf16[256,8,64]{0,2,1:T(8,128)(2,1)S(1)} %bitcast.319, f32[384,256,8]{1,0,2:T(8,128)S(1)} %get-tuple-element.101, f32[8,256]{1,0:T(8,128)S(1)} %exponential_add_fusion.3, f32[8,256]{1,0:T(8,128)S(1)} %broadcast_maximum_fusion.3, pred[256,384]{0,1:T(8,128)(4,1)S(1)} %fusion.44), kind=kOutput, calls=%fused_computation.54 | convolution fusion | flops 105381888 | bytes 3620864 | tf_op jit(solution)/shard_map/grl,rgd->ld/dot_general | solution.py:139
  49.1 1.2 %fusion.7 = bf16[8,256,384]{1,2,0:T(8,128)(2,1)S(1)} fusion(bf16[256,8,64]{0,2,1:T(8,128)(2,1)S(1)} %bitcast.320, f32[8,256]{1,0:T(8,128)S(1)} %get-tuple-element.82, bf16[256,256]{0,1:T(8,128)(2,1)S(1)} %get-tuple-element.89, bf16[128,256]{0,1:T(8,128)(2,1)S(1)} %get-tuple-element.95, f32[8,256]{1,0:T(8,128)S(1)} %exponential_add_fusion.3, ...), kind=kOutput, calls=%fused_computation.11 | convolution fusion | flops 107053056 | bytes 5300224 | tf_op jit(solution)/shard_map/rgd,ld->grl/dot_general | solution.py:125
  59.7 6.2 %collective-permute-start.3 = (f32[128,512]{0,1:T(8,128)}, f32[128,512]{0,1:T(8,128)}, u32[]{:S(2)}, u32[]{:S(2)}) collective-permute-start(f32[128,512]{0,1:T(8,128)} %pad_maximum_fusion.2), channel_id=1, source_target_pairs={{1,0},{2,1},{3,2},{5,4},{6,5},{7,6},{9,8},{10,9},{11,10},{13,12},{... | collective-permute-start | bytes 786440 | tf_op jit(solution)/shard_map/ppermute | solution.py:28
  66.2 1.0 %concatenate.125 = bf16[16,16,512]{2,1,0:T(8,128)(2,1)} reshape(bf16[256,8,64]{2,1,0:T(8,128)(2,1)S(1)} %copy.64) | data formatting | bytes 524288 | tf_op jit(solution)/shard_map/concatenate | solution.py:151
  73.9 3.0 %collective-permute-start.2 = (bf16[1,16,2048]{2,1,0:T(8,128)(2,1)S(1)}, bf16[1,16,2048]{2,1,0:T(8,128)(2,1)S(1)}, u32[]{:S(2)}, u32[]{:S(2)}) collective-permute-start(bf16[1,16,2048]{2,1,0:T(8,128)(2,1)S(1)} %broadcast_select_fusion.1), channel_id=1, source_target_pairs={{0,8},{8,0},{4,12},{12,4},{1,9},{9,1},{5,13},{13,5},{2,10},{10,2},... | collective-permute-start | bytes 196616 | tf_op jit(solution)/shard_map/ppermute | solution.py:22
  81.8 1.2 %constant_dynamic-update-slice_fusion.10 = bf16[256,2560]{1,0:T(8,128)(2,1)S(1)} fusion(bf16[256,2560]{1,0:T(8,128)(2,1)S(1)} %constant_dynamic-update-slice_fusion.11, bf16[256,512]{1,0:T(8,128)(2,1)} %copy.82), kind=kLoop, calls=%fused_computation.147 | loop fusion | bytes 524288
  85.1 1.4 %maximum_select_fusion.1 = bf16[1,256,2048]{2,1,0:T(8,128)(2,1)} fusion(bf16[1,256,512]{2,1,0:T(8,128)(2,1)S(1)} %copy-done.3, bf16[1,256,512]{2,1,0:T(8,128)(2,1)S(1)} %copy-done.5, bf16[1,256,512]{2,1,0:T(8,128)(2,1)S(1)} %copy-done.4, bf16[1,256,512]{2,1,0:T(8,128)(2,1)S(1)} %copy-done.2, pred[256]{0:T(512)(128)(4,1)S(1)} %broadcast_in_dim.156, ...), kind=kLoop, calls=%fused_computation.64 | loop fusion | flops 5242880 | bytes 3146240 | tf_op jit(solution)/shard_map/jit(_where)/select_n | solution.py:58
  90.2 5.2 %collective-permute-done.4 = bf16[1,16,2560]{2,1,0:T(8,128)(2,1)S(1)} collective-permute-done((bf16[1,16,2560]{2,1,0:T(8,128)(2,1)S(1)}, bf16[1,16,2560]{2,1,0:T(8,128)(2,1)S(1)}, u32[]{:S(2)}, u32[]{:S(2)}) %collective-permute-start.4) | collective-permute-done | bytes 81952 | tf_op jit(solution)/shard_map/ppermute | solution.py:22
  96.4 1.1 %slice_bitcast_fusion = bf16[1,256,2048]{2,1,0:T(8,128)(2,1)} fusion(bf16[256,2560]{1,0:T(8,128)(2,1)S(1)} %fusion.20), kind=kLoop, calls=%fused_computation.63 | loop fusion | bytes 2097152 | tf_op jit(solution)/shard_map/broadcast_in_dim | solution.py:155
  (114 shorter events, 37.9 us)
Async XLA Ops:
  0.6 12.2 %copy-start = (bf16[1,256,2048]{2,1,0:T(8,128)(2,1)S(1)}, bf16[1,256,2048]{2,1,0:T(8,128)(2,1)}, u32[]{:S(2)}) copy-start(bf16[1,256,2048]{2,1,0:T(8,128)(2,1)} %param.11) | copy-start | bytes 3145732
  0.6 12.8 %copy-start.1 = (bf16[1,256,2048]{2,1,0:T(8,128)(2,1)S(1)}, bf16[1,256,2048]{2,1,0:T(8,128)(2,1)}, u32[]{:S(2)}) copy-start(bf16[1,256,2048]{2,1,0:T(8,128)(2,1)} %param.14) | copy-start | bytes 3145732
  4.9 10.1 %copy-start.10 = (s32[1,1024]{1,0:T(1,128)S(1)}, s32[1,1024]{1,0:T(1,128)}, u32[]{:S(2)}) copy-start(s32[1,1024]{1,0:T(1,128)} %param.16) | copy-start | bytes 12292
  5.0 10.3 %copy-start.9 = (f32[32]{0:T(128)S(1)}, f32[32]{0:T(128)}, u32[]{:S(2)}) copy-start(f32[32]{0:T(128)} %param.15) | copy-start | bytes 388
  6.6 9.2 %collective-permute-start = (bf16[1,16,4608]{2,1,0:T(8,128)(2,1)}, bf16[1,16,4608]{2,1,0:T(8,128)(2,1)S(1)}, u32[]{:S(2)}, u32[]{:S(2)}) collective-permute-start(bf16[1,16,4608]{2,1,0:T(8,128)(2,1)} %broadcast_select_fusion), channel_id=1, source_target_pairs={{0,8},{8,0},{4,12},{12,4},{1,9},{9,1},{5,13},{13,5},{2,10},{10,2},... | collective-permute-start | bytes 442376 | tf_op jit(solution)/shard_map/ppermute | solution.py:22
  15.8 0.7 copy-start.7
  22.6 3.3 %collective-permute-start.1 = (bf16[128,512]{0,1:T(8,128)(2,1)S(1)}, bf16[128,512]{0,1:T(8,128)(2,1)S(1)}, u32[]{:S(2)}, u32[]{:S(2)}) collective-permute-start(bf16[128,512]{0,1:T(8,128)(2,1)S(1)} %slice.229), channel_id=1, source_target_pairs={{0,1},{1,2},{2,3},{4,5},{5,6},{6,7},{8,9},{9,10},{10,11},{12,13},{... | collective-permute-start | bytes 393224 | tf_op jit(solution)/shard_map/ppermute | solution.py:28
  59.7 26.8 %collective-permute-start.3 = (f32[128,512]{0,1:T(8,128)}, f32[128,512]{0,1:T(8,128)}, u32[]{:S(2)}, u32[]{:S(2)}) collective-permute-start(f32[128,512]{0,1:T(8,128)} %pad_maximum_fusion.2), channel_id=1, source_target_pairs={{1,0},{2,1},{3,2},{5,4},{6,5},{7,6},{9,8},{10,9},{11,10},{13,12},{... | collective-permute-start | bytes 786440 | tf_op jit(solution)/shard_map/ppermute | solution.py:28
  73.8 11.3 %copy-start.2 = (bf16[1,256,512]{2,1,0:T(8,128)(2,1)S(1)}, bf16[1,256,512]{2,1,0:T(8,128)(2,1)}, u32[]{:S(2)}) copy-start(bf16[1,256,512]{2,1,0:T(8,128)(2,1)} %copy.59) | copy-start | bytes 786436
  73.8 11.3 %copy-start.3 = (bf16[1,256,512]{2,1,0:T(8,128)(2,1)S(1)}, bf16[1,256,512]{2,1,0:T(8,128)(2,1)}, u32[]{:S(2)}) copy-start(bf16[1,256,512]{2,1,0:T(8,128)(2,1)} %copy.62) | copy-start | bytes 786436
  73.8 11.3 %copy-start.4 = (bf16[1,256,512]{2,1,0:T(8,128)(2,1)S(1)}, bf16[1,256,512]{2,1,0:T(8,128)(2,1)}, u32[]{:S(2)}) copy-start(bf16[1,256,512]{2,1,0:T(8,128)(2,1)} %copy.60) | copy-start | bytes 786436
  73.9 11.3 %copy-start.5 = (bf16[1,256,512]{2,1,0:T(8,128)(2,1)S(1)}, bf16[1,256,512]{2,1,0:T(8,128)(2,1)}, u32[]{:S(2)}) copy-start(bf16[1,256,512]{2,1,0:T(8,128)(2,1)} %copy.61) | copy-start | bytes 786436
  73.9 11.1 %collective-permute-start.2 = (bf16[1,16,2048]{2,1,0:T(8,128)(2,1)S(1)}, bf16[1,16,2048]{2,1,0:T(8,128)(2,1)S(1)}, u32[]{:S(2)}, u32[]{:S(2)}) collective-permute-start(bf16[1,16,2048]{2,1,0:T(8,128)(2,1)S(1)} %broadcast_select_fusion.1), channel_id=1, source_target_pairs={{0,8},{8,0},{4,12},{12,4},{1,9},{9,1},{5,13},{13,5},{2,10},{10,2},... | collective-permute-start | bytes 196616 | tf_op jit(solution)/shard_map/ppermute | solution.py:22
  80.8 5.7 %copy-start.6 = (bf16[256,256]{0,1:T(8,128)(2,1)S(1)}, bf16[256,256]{0,1:T(8,128)(2,1)}, u32[]{:S(2)}) copy-start(bf16[256,256]{0,1:T(8,128)(2,1)} %slice.254) | copy-start | bytes 393220
  81.8 3.1 %copy-start.8 = (bf16[16,16,2560]{2,1,0:T(8,128)(2,1)}, bf16[16,16,2560]{2,1,0:T(8,128)(2,1)S(1)}, u32[]{:S(2)}) copy-start(bf16[16,16,2560]{2,1,0:T(8,128)(2,1)S(1)} %constant_dynamic-update-slice_fusion.2) | copy-start | bytes 3932164
  90.0 5.4 %collective-permute-start.4 = (bf16[1,16,2560]{2,1,0:T(8,128)(2,1)S(1)}, bf16[1,16,2560]{2,1,0:T(8,128)(2,1)S(1)}, u32[]{:S(2)}, u32[]{:S(2)}) collective-permute-start(bf16[1,16,2560]{2,1,0:T(8,128)(2,1)S(1)} %dynamic-slice_select_fusion), channel_id=1, source_target_pairs={{0,8},{8,0},{4,12},{12,4},{1,9},{9,1},{5,13},{13,5},{2,10},{10,2},... | collective-permute-start | bytes 245768 | tf_op jit(solution)/shard_map/ppermute | solution.py:22
where the time goes:
time: 98.1 us; the launch traced here: 97.5 us
  local copies, waits for them, and re-layouts  37.8 us (39%)
  matrix products  21.9 us (22%)
  other arithmetic  14.1 us (14%)
  starting transfers between devices  12.9 us (13%)
  waiting for transfers between devices  7.58 us (8%)
  between operations  3.15 us (3%)
    unnamed x36, local copies, waits for them, and re-layouts  14.5 us
    concatenate x10, local copies, waits for them, and re-layouts, shards(): gradients = trade(jnp.concatenate([pack_dq, pack_dk, pack_dv], axis=1))  8.2 us
    ppermute x2, starting transfers between devices, shifted(): lax.ppermute(value, axis, [(source, source + steps) for source in range(i...  7.45 us
    ppermute x3, waiting for transfers between devices, swapped(): return lax.ppermute(block, axis, route)  5.64 us
    ppermute x3, starting transfers between devices, swapped(): return lax.ppermute(block, axis, route)  5.5 us
    dot_general x4, matrix products, shards(): jnp.einsum('rgd,ld->grl', grad_group, value_group, preferred_element_type...  4.91 us
    concatenate x8, local copies, waits for them, and re-layouts, shards(): pack_out = jnp.concatenate(out_parts, axis=1)  4.66 us
    dot_general x4, matrix products, shards(): jnp.einsum('grl,ld->rgd', probs_b, value_group, preferred_element_type=jn...  4.39 us
  transfers between devices with their start and end apart: 5, of which 3 were waited for; matrix products, arithmetic and copies ran while one was open for 24% of the time, Pallas kernels for 0%

commit v1 on v0

v1 whole, which is shorter than its diff:
```python
import functools
import math

import jax
import jax.numpy as jnp
from jax import lax
from jax.experimental import pallas as pl
from jax.experimental.pallas import tpu as pltpu
from jax.sharding import PartitionSpec as P

KEY_VALUE_HEADS = 4
HEAD_SIZE = 64
WINDOW = 128
MESH = pl.DeviceIdType.MESH
F32 = jnp.float32
BF16 = jnp.bfloat16
NT = (((1,), (1,)), ((), ()))
NN = (((1,), (0,)), ((), ()))
TN = (((0,), (0,)), ((), ()))


def mm(a, b, dims):
    return lax.dot_general(a, b, dims, preferred_element_type=F32)


def kernel(
    dims,
    flags, sinks, docs, q_hbm, k_hbm, v_hbm, g_hbm,
    out_hbm, dq_hbm, dk_hbm, dv_hbm,
    kv, qv, gv, qp, gp, ov, dqv, dkv, dkv_t,
    kk, vv, bias, mask, hmask, scores, probs, probs_b, ds_b,
    kv_send, kv_in, kv_diag, tail_in, fl_send, fl_in,
    qg_send, qg_in, hg_send, hg_in, og_send, og_in, dkv_send, dkv_in,
    load_sem, qload_sem, gload_sem, store_sem, sem_kv, sem_diag, sem_tail, sem_fl,
    sem_qg, sem_hg, sem_og, sem_dkv,
):
    rows, groups, width, pairs, blocks, blk = dims
    chunks = rows // WINDOW
    kvw = groups * HEAD_SIZE
    dp, ctx = lax.axis_index("dp"), lax.axis_index("ctx")
    dps, ctxs = lax.axis_size("dp"), lax.axis_size("ctx")
    partner = lax.rem(dp + dps // 2, dps)
    right = lax.rem(ctx + 1, ctxs)
    left = lax.rem(ctx + ctxs - 1, ctxs)

    def send(src, dst, sems, where):
        return pltpu.make_async_remote_copy(
            src_ref=src, dst_ref=dst, send_sem=sems.at[0], recv_sem=sems.at[1],
            device_id=where, device_id_type=MESH,
        )

    k_load = pltpu.make_async_copy(k_hbm, kv.at[:, pl.ds(0, kvw)], load_sem.at[0])
    v_load = pltpu.make_async_copy(v_hbm, kv.at[:, pl.ds(kvw, kvw)], load_sem.at[1])
    k_load.start()
    v_load.start()

    def q_load(i):
        return pltpu.make_async_copy(q_hbm.at[:, pl.ds(i * width, width)], qv.at[i], qload_sem.at[i])

    def g_load(i):
        return pltpu.make_async_copy(g_hbm.at[:, pl.ds(i * width, width)], gv.at[i], gload_sem.at[i])

    for i in range(groups):
        q_load(i).start()
        g_load(i).start()

    peers = (
        {"dp": partner}, {"ctx": right}, {"ctx": left},
        {"dp": partner, "ctx": right}, {"dp": partner, "ctx": left},
    )
    barrier = pltpu.get_barrier_semaphore()
    for peer in peers:
        pl.semaphore_signal(barrier, inc=1, device_id=peer, device_id_type=MESH)

    for j in range(blocks):
        value = flags[j].astype(F32)
        mask[j * blk : (j + 1) * blk, :] = jnp.full((blk, 128), value, F32).astype(BF16)

    def picked(ref, lead, lanes):
        block = jnp.zeros((blk, 128), BF16)
        for j in range(blocks):
            at = slice(j * blk, (j + 1) * blk)
            block = jnp.where(mask[at, :] > 0, ref[lead + (at, lanes)], block)
        return block

    tail_blocks = WINDOW // blk
    line = lax.broadcasted_iota(jnp.int32, (tail_blocks, 128), 0)
    tail_flags = jnp.zeros((tail_blocks, 128), F32)
    for j in range(tail_blocks):
        value = flags[blocks - tail_blocks + j].astype(F32)
        tail_flags = jnp.where(line == j, value, tail_flags)
    fl_send[...] = tail_flags

    k_load.wait()
    v_load.wait()
    for a in range(groups):
        lanes = slice(a * 128, (a + 1) * 128)
        kv_send[:, lanes] = picked(kv, (), lanes)
    pl.semaphore_wait(barrier, len(peers))
    kv_copy = send(kv_send, kv_in, sem_kv, {"dp": partner})
    diag_copy = send(kv_send, kv_diag, sem_diag, {"dp": partner, "ctx": right})
    fl_copy = send(fl_send, fl_in, sem_fl, {"ctx": right})
    tail_copy = send(kv.at[pl.ds(rows - WINDOW, WINDOW), :], tail_in, sem_tail, {"ctx": right})
    kv_copy.start()
    diag_copy.start()
    fl_copy.start()
    tail_copy.start()

    def qg_copy(i):
        return send(qg_send.at[i], qg_in.at[i], sem_qg.at[i], {"dp": partner})

    for i in range(groups):
        q_load(i).wait()
        g_load(i).wait()
        for a in range(pairs):
            lanes = slice(a * 128, (a + 1) * 128)
            qg_send[i, :, lanes] = picked(qv, (i,), lanes)
            qg_send[i, :, width + a * 128 : width + (a + 1) * 128] = picked(gv, (i,), lanes)
        qg_copy(i).start()

    offset = ctx * rows
    near = jnp.maximum(offset - WINDOW, 0)
    halo_docs = docs[:, pl.ds(pl.multiple_of(near, 128), WINDOW)]
    halo_docs = jnp.where(ctx == 0, -1, halo_docs)
    own_docs = docs[:, pl.ds(pl.multiple_of(offset, 128), rows)]
    key_docs = jnp.concatenate([halo_docs, own_docs], axis=1).astype(F32)
    dist = (
        lax.broadcasted_iota(jnp.int32, (WINDOW, 2 * WINDOW), 0)
        + WINDOW
        - lax.broadcasted_iota(jnp.int32, (WINDOW, 2 * WINDOW), 1)
    )
    near_enough = (dist >= 0) & (dist < WINDOW)
    for c in range(chunks):
        lanes = jnp.broadcast_to(key_docs[:, (c + 1) * WINDOW : (c + 2) * WINDOW], (WINDOW, WINDOW))
        turned = jnp.transpose(lanes)
        column = jnp.concatenate([turned, turned], axis=1)
        these = jnp.broadcast_to(key_docs[:, c * WINDOW : (c + 2) * WINDOW], (WINDOW, 2 * WINDOW))
        bias[c] = jnp.where((column == these) & near_enough, F32(0.0), F32(-1e30))

    kv_copy.wait_recv()
    diag_copy.wait_recv()
    fl_copy.wait_recv()
    tail_copy.wait_recv()
    hmask[...] = jnp.broadcast_to(fl_in[...][:, None, :], (tail_blocks, blk, 128)).reshape(WINDOW, 128).astype(BF16)

    def merged(mask_ref, first, count, block, own):
        spread = jnp.concatenate([block] * (count // blk), axis=0)
        return jnp.where(mask_ref[first : first + count, :] > 0, spread, own)

    source = lax.broadcasted_iota(jnp.int32, (128, 256), 0)
    target = lax.broadcasted_iota(jnp.int32, (128, 256), 1)
    half = HEAD_SIZE
    scale = 1.0 / math.sqrt(HEAD_SIZE)
    for pair in range(2 * groups // 2):
        at = pair * 128
        halo = merged(hmask, 0, WINDOW, kv_diag[:, at : at + 128], tail_in[:, at : at + 128])
        own = merged(mask, 0, rows, kv_in[:, at : at + 128], kv[:, at : at + 128])
        both = jnp.concatenate([halo, own], axis=0)
        is_key = at < kvw
        for parity in range(2):
            group = (at % kvw) // half + parity
            place = source - parity * half
            valid = (place >= 0) & (place < half)
            pick = valid & ((target == place) | (target == place + 128 + half))
            weight = jnp.where(pick, F32(scale if is_key else 1.0), F32(0.0)).astype(BF16)
            laid = mm(both, weight, NN).astype(BF16)
            ref = kk if is_key else vv
            for c in range(chunks):
                ref[group, c, : 2 * WINDOW, :] = laid[c * WINDOW : (c + 2) * WINDOW, :128]
                ref[group, c, 2 * WINDOW :, :] = laid[c * WINDOW : (c + 2) * WINDOW, 128:]

    def hg_copy(i):
        return send(hg_send.at[i], hg_in.at[i], sem_hg.at[i], {"ctx": left})

    def og_copy(i):
        return send(og_send.at[i], og_in.at[i], sem_og.at[i], {"dp": partner})

    low = lax.broadcasted_iota(jnp.int32, (pairs * WINDOW, 128), 1) < half

    def group_step(i, carry):
        qg_copy(i).wait_recv()
        for c in range(chunks):
            for a in range(pairs):
                lanes = slice(a * 128, (a + 1) * 128)
                mine = slice(c * WINDOW, (c + 1) * WINDOW)
                there = slice(width + a * 128, width + (a + 1) * 128)
                qp[c, a * WINDOW : (a + 1) * WINDOW, :] = merged(
                    mask, c * WINDOW, WINDOW, qg_in[i, :, lanes], qv[i, mine, lanes]
                )
                gp[c, a * WINDOW : (a + 1) * WINDOW, :] = merged(
                    mask, c * WINDOW, WINDOW, qg_in[i, :, there], gv[i, mine, lanes]
                )
        for c in range(chunks):
            q_c, g_c, k_c, v_c = qp[c], gp[c], kk[i, c], vv[i, c]
            scores[...] = mm(q_c, k_c, NT)
            for a in range(pairs):
                for parity in range(2):
                    at_r = slice(a * WINDOW, (a + 1) * WINDOW)
                    at_c = slice(parity * 2 * WINDOW, (parity + 1) * 2 * WINDOW)
                    sink = sinks[i * (2 * pairs) + 2 * a + parity]
                    s = scores[at_r, at_c] + bias[c]
                    top = jnp.maximum(jnp.max(s, axis=1, keepdims=True), sink)
                    e = jnp.exp(s - top)
                    total = jnp.exp(sink - top) + jnp.sum(e, axis=1, keepdims=True)
                    p = e * (1.0 / total)
                    probs[at_r, at_c] = p
                    probs_b[at_r, at_c] = p.astype(BF16)
            p_c = probs_b[...]
            out = mm(p_c, v_c, NN).astype(BF16)
            product = g_c.astype(F32) * out.astype(F32)
            even = jnp.sum(jnp.where(low, product, 0.0), axis=1, keepdims=True)
            odd = jnp.sum(jnp.where(low, 0.0, product), axis=1, keepdims=True)
            scores[...] = mm(g_c, v_c, NT)
            for parity, dot in ((0, even), (1, odd)):
                at_c = slice(parity * 2 * WINDOW, (parity + 1) * 2 * WINDOW)
                ds_b[:, at_c] = (probs[:, at_c] * (scores[:, at_c] - dot)).astype(BF16)
            ds = ds_b[...]
            dq = mm(ds, k_c, NN).astype(BF16)
            mine = slice(c * WINDOW, (c + 1) * WINDOW)
            for a in range(pairs):
                lanes = slice(a * 128, (a + 1) * 128)
                ov[i, mine, lanes] = out[a * WINDOW : (a + 1) * WINDOW]
                dqv[i, mine, lanes] = dq[a * WINDOW : (a + 1) * WINDOW]
            dkt = mm(q_c, ds, TN) * scale
            dvt = mm(g_c, p_c, TN)
            dkt = dkt[:half, : 2 * WINDOW] + dkt[half:, 2 * WINDOW :]
            dvt = dvt[:half, : 2 * WINDOW] + dvt[half:, 2 * WINDOW :]
            if c == 0:
                hg_send[i, :half, :] = dkt[:, :WINDOW]
                hg_send[i, half:, :] = dvt[:, :WINDOW]
                hg_copy(i).start()
            else:
                old = slice((c - 1) * WINDOW, c * WINDOW)
                dkv_t[i, :half, old] = dkv_t[i, :half, old] + dkt[:, :WINDOW]
                dkv_t[i, half:, old] = dkv_t[i, half:, old] + dvt[:, :WINDOW]
            dkv_t[i, :half, mine] = dkt[:, WINDOW:]
            dkv_t[i, half:, mine] = dvt[:, WINDOW:]
        for a in range(pairs):
            lanes = slice(a * 128, (a + 1) * 128)
            og_send[i, :, lanes] = picked(ov, (i,), lanes)
            og_send[i, :, width + a * 128 : width + (a + 1) * 128] = picked(dqv, (i,), lanes)
        og_copy(i).start()
        return carry

    lax.fori_loop(0, groups, group_step, 0)

    for i in range(groups):
        hg_copy(i).wait_recv()
    last = slice(rows - WINDOW, rows)
    for part in range(2):
        for pair in range(groups // 2):
            stack = []
            for i in (2 * pair, 2 * pair + 1):
                at_h = slice(part * half, (part + 1) * half)
                kept = dkv_t[i, at_h, : rows - WINDOW]
                end = dkv_t[i, at_h, last] + hg_in[i, at_h, :]
                stack.append(jnp.concatenate([kept, end], axis=1))
            both = jnp.concatenate(stack, axis=0)
            at = part * kvw + pair * 128
            dkv[:, at : at + 128] = jnp.transpose(both).astype(BF16)
    for a in range(groups):
        lanes = slice(a * 128, (a + 1) * 128)
        dkv_send[:, lanes] = picked(dkv, (), lanes)
    dkv_copy = send(dkv_send, dkv_in, sem_dkv, {"dp": partner})
    dkv_copy.start()

    def out_store(i):
        return pltpu.make_async_copy(ov.at[i], out_hbm.at[:, pl.ds(i * width, width)], qload_sem.at[i])

    def dq_store(i):
        return pltpu.make_async_copy(dqv.at[i], dq_hbm.at[:, pl.ds(i * width, width)], gload_sem.at[i])

    for i in range(groups):
        og_copy(i).wait_recv()
        for a in range(pairs):
            lanes = slice(a * 128, (a + 1) * 128)
            there = slice(width + a * 128, width + (a + 1) * 128)
            ov[i, :, lanes] = merged(mask, 0, rows, og_in[i, :, lanes], ov[i, :, lanes])
            dqv[i, :, lanes] = merged(mask, 0, rows, og_in[i, :, there], dqv[i, :, lanes])
        out_store(i).start()
        dq_store(i).start()

    dkv_copy.wait_recv()
    for pair in range(groups):
        lanes = slice(pair * 128, (pair + 1) * 128)
        dkv[:, lanes] = merged(mask, 0, rows, dkv_in[:, lanes], dkv[:, lanes])
    dk_store = pltpu.make_async_copy(dkv.at[:, pl.ds(0, kvw)], dk_hbm, store_sem.at[0])
    dv_store = pltpu.make_async_copy(dkv.at[:, pl.ds(kvw, kvw)], dv_hbm, store_sem.at[1])
    dk_store.start()
    dv_store.start()

    kv_copy.wait_send()
    diag_copy.wait_send()
    fl_copy.wait_send()
    tail_copy.wait_send()
    dkv_copy.wait_send()
    for i in range(groups):
        qg_copy(i).wait_send()
        hg_copy(i).wait_send()
        og_copy(i).wait_send()
        out_store(i).wait()
        dq_store(i).wait()
    dk_store.wait()
    dv_store.wait()


def shards(queries, keys, values, grad_out, sinks, doc_ids, swap_flags):
    rows = queries.shape[1]
    full = queries.shape[2]
    kvw = keys.shape[2]
    groups = KEY_VALUE_HEADS
    width = full // groups
    pairs = width // 128
    blocks = swap_flags.shape[2]
    blk = rows // blocks
    chunks = rows // WINDOW
    dims = (rows, groups, width, pairs, blocks, blk)
    vm = pltpu.VMEM
    dma = pltpu.SemaphoreType.DMA
    stack = pairs * WINDOW
    span = 4 * WINDOW
    scratch = [
        vm((rows, 2 * kvw), BF16),
        vm((groups, rows, width), BF16), vm((groups, rows, width), BF16),
        vm((chunks, stack, 128), BF16), vm((chunks, stack, 128), BF16),
        vm((groups, rows, width), BF16), vm((groups, rows, width), BF16),
        vm((rows, 2 * kvw), BF16), vm((groups, 2 * HEAD_SIZE, rows), F32),
        vm((groups, chunks, span, 128), BF16), vm((groups, chunks, span, 128), BF16),
        vm((chunks, WINDOW, 2 * WINDOW), F32), vm((rows, 128), BF16), vm((WINDOW, 128), BF16),
        vm((stack, span), F32), vm((stack, span), F32), vm((stack, span), BF16), vm((stack, span), BF16),
        vm((blk, 2 * kvw), BF16), vm((blk, 2 * kvw), BF16), vm((blk, 2 * kvw), BF16),
        vm((WINDOW, 2 * kvw), BF16), vm((WINDOW // blk, 128), F32), vm((WINDOW // blk, 128), F32),
        vm((groups, blk, 2 * width), BF16), vm((groups, blk, 2 * width), BF16),
        vm((groups, 2 * HEAD_SIZE, WINDOW), F32), vm((groups, 2 * HEAD_SIZE, WINDOW), F32),
        vm((groups, blk, 2 * width), BF16), vm((groups, blk, 2 * width), BF16),
        vm((blk, 2 * kvw), BF16), vm((blk, 2 * kvw), BF16),
        dma((2,)), dma((groups,)), dma((groups,)), dma((2,)),
        dma((2,)), dma((2,)), dma((2,)), dma((2,)),
        dma((groups, 2)), dma((groups, 2)), dma((groups, 2)), dma((2,)),
    ]
    hbm = pl.BlockSpec(memory_space=pl.ANY)
    smem = pl.BlockSpec(memory_space=pltpu.SMEM)
    big = jax.ShapeDtypeStruct((rows, full), BF16)
    small = jax.ShapeDtypeStruct((rows, kvw), BF16)
    results = pl.pallas_call(
        functools.partial(kernel, dims),
        out_shape=(big, big, small, small),
        in_specs=[smem, smem, pl.BlockSpec(memory_space=pltpu.VMEM), hbm, hbm, hbm, hbm],
        out_specs=(hbm, hbm, hbm, hbm),
        scratch_shapes=scratch,
        compiler_params=pltpu.CompilerParams(
            collective_id=0, has_side_effects=True, vmem_limit_bytes=48 * 1024 * 1024
        ),
        cost_estimate=pl.CostEstimate(
            flops=10 * rows * full * 2 * WINDOW, bytes_accessed=8 * rows * full, transcendentals=0
        ),
    )(swap_flags[0, 0], sinks, doc_ids, queries[0], keys[0], values[0], grad_out[0])
    return tuple(result[None] for result in results)


def solution(mesh):
    rows_spec = P(("groups", "dp"), "ctx", None)
    in_specs = (rows_spec, rows_spec, rows_spec, rows_spec, P(), P(("groups", "dp"), None), rows_spec)
    return jax.shard_map(
        shards, mesh=mesh, in_specs=in_specs, out_specs=(rows_spec,) * 4, check_vma=False
    )
```

time: 98.1 us -> 37.1 us (0.38)
  the two profiles are of different devices: /device:TPU:11 before, /device:TPU:13 now
where the time goes in v1:
time: 37.1 us; the launch traced here: 36.9 us
  Pallas kernels  28 us (75%)
  local copies, waits for them, and re-layouts  8.18 us (22%)
  between operations  0.67 us (2%)
    pallas_call x1, Pallas kernels, shards(): pl.pallas_call(functools.partial(kernel, dims), out_shape=(big, big, smal...  28 us
    unnamed x18, local copies, waits for them, and re-layouts  8.18 us

profile of v1, /device:TPU:13, one launch (start us, length us, event | category | flops | bytes accessed | tf_op | source)
XLA Modules:
  0.0 36.9 jit_solution(12163157937939915512)
XLA Ops:
  0.6 0.0 copy-start.4
  0.6 0.0 copy-start.5
  0.7 0.0 copy-start.6
  0.7 0.7 %copy-done.4 = s32[1,1024]{1,0:T(1,128)S(1)} copy-done((s32[1,1024]{1,0:T(1,128)S(1)}, s32[1,1024]{1,0:T(1,128)}, u32[]{:S(2)}) %copy-start.4) | copy-done | bytes 4120
  1.3 0.0 copy-done.5
  1.3 0.0 copy-done.6
  1.3 0.0 copy-start
  1.3 1.2 %copy-done = bf16[1,256,2048]{2,1,0:T(8,128)(2,1)S(1)} copy-done((bf16[1,256,2048]{2,1,0:T(8,128)(2,1)S(1)}, bf16[1,256,2048]{2,1,0:T(8,128)(2,1)}, u32[]{:S(2)}) %copy-start) | copy-done | bytes 1048600
  2.6 0.0 copy-start.1
  2.6 1.2 %copy-done.1 = bf16[1,256,2048]{2,1,0:T(8,128)(2,1)S(1)} copy-done((bf16[1,256,2048]{2,1,0:T(8,128)(2,1)S(1)}, bf16[1,256,2048]{2,1,0:T(8,128)(2,1)}, u32[]{:S(2)}) %copy-start.1) | copy-done | bytes 1048600
  3.8 0.0 copy-start.2
  3.8 0.9 %copy-done.2 = bf16[1,256,256]{2,1,0:T(8,128)(2,1)S(1)} copy-done((bf16[1,256,256]{2,1,0:T(8,128)(2,1)S(1)}, bf16[1,256,256]{2,1,0:T(8,128)(2,1)}, u32[]{:S(2)}) %copy-start.2) | copy-done | bytes 131096
  4.7 0.0 copy-start.3
  4.7 0.9 %copy-done.3 = bf16[1,256,256]{2,1,0:T(8,128)(2,1)S(1)} copy-done((bf16[1,256,256]{2,1,0:T(8,128)(2,1)S(1)}, bf16[1,256,256]{2,1,0:T(8,128)(2,1)}, u32[]{:S(2)}) %copy-start.3) | copy-done | bytes 131096
  5.6 28.0 %shard_map.102 = (bf16[256,2048]{1,0:T(8,128)(2,1)S(1)}, bf16[256,2048]{1,0:T(8,128)(2,1)S(1)}, bf16[256,256]{1,0:T(8,128)(2,1)S(1)}, bf16[256,256]{1,0:T(8,128)(2,1)S(1)}) custom-call(s32[16]{0:T(128)S(1)} %bitcast.17, f32[32]{0:T(128)S(1)} %copy-done.6, s32[1,1024]{1,0:T(1,128)S(1)} %copy-done.4, bf16[256,2048]{1,0:T(8,128)(2,1)S(1)} %bitcast.13, ...), custom_call_target="tpu_custom_call" | custom-call | flops 1342177280 | bytes 4194304 | tf_op jit(solution)/shard_map/pallas_call | solution.py:345
  33.6 1.0 %copy.15 = bf16[1,256,2048]{2,1,0:T(8,128)(2,1)} copy(bf16[1,256,2048]{2,1,0:T(8,128)(2,1)S(1)} %bitcast.10) | data formatting | bytes 2097152
  34.6 1.0 %copy.16 = bf16[1,256,2048]{2,1,0:T(8,128)(2,1)} copy(bf16[1,256,2048]{2,1,0:T(8,128)(2,1)S(1)} %bitcast.9) | data formatting | bytes 2097152
  35.6 0.7 %copy.17 = bf16[1,256,256]{2,1,0:T(8,128)(2,1)} copy(bf16[1,256,256]{2,1,0:T(8,128)(2,1)S(1)} %bitcast.12) | data formatting | bytes 262144
  36.2 0.7 %copy.18 = bf16[1,256,256]{2,1,0:T(8,128)(2,1)} copy(bf16[1,256,256]{2,1,0:T(8,128)(2,1)S(1)} %bitcast.11) | data formatting | bytes 262144
Async XLA Ops:
  0.6 0.7 %copy-start.4 = (s32[1,1024]{1,0:T(1,128)S(1)}, s32[1,1024]{1,0:T(1,128)}, u32[]{:S(2)}) copy-start(s32[1,1024]{1,0:T(1,128)} %docs.1) | copy-start | bytes 12292
  0.6 0.7 %copy-start.5 = (s32[1,1,16]{2,1,0:T(1,128)S(1)}, s32[1,1,16]{2,1,0:T(1,128)}, u32[]{:S(2)}) copy-start(s32[1,1,16]{2,1,0:T(1,128)} %param.13) | copy-start | bytes 196
  0.7 0.7 %copy-start.6 = (f32[32]{0:T(128)S(1)}, f32[32]{0:T(128)}, u32[]{:S(2)}) copy-start(f32[32]{0:T(128)} %sinks.1) | copy-start | bytes 388
  1.3 1.2 %copy-start = (bf16[1,256,2048]{2,1,0:T(8,128)(2,1)S(1)}, bf16[1,256,2048]{2,1,0:T(8,128)(2,1)}, u32[]{:S(2)}) copy-start(bf16[1,256,2048]{2,1,0:T(8,128)(2,1)} %param.7) | copy-start | bytes 3145732
  2.6 1.2 %copy-start.1 = (bf16[1,256,2048]{2,1,0:T(8,128)(2,1)S(1)}, bf16[1,256,2048]{2,1,0:T(8,128)(2,1)}, u32[]{:S(2)}) copy-start(bf16[1,256,2048]{2,1,0:T(8,128)(2,1)} %param.10) | copy-start | bytes 3145732
  3.8 0.9 %copy-start.2 = (bf16[1,256,256]{2,1,0:T(8,128)(2,1)S(1)}, bf16[1,256,256]{2,1,0:T(8,128)(2,1)}, u32[]{:S(2)}) copy-start(bf16[1,256,256]{2,1,0:T(8,128)(2,1)} %param.8) | copy-start | bytes 393220
  4.7 0.9 %copy-start.3 = (bf16[1,256,256]{2,1,0:T(8,128)(2,1)S(1)}, bf16[1,256,256]{2,1,0:T(8,128)(2,1)}, u32[]{:S(2)}) copy-start(bf16[1,256,256]{2,1,0:T(8,128)(2,1)} %param.9) | copy-start | bytes 393220

commit v2 on v1

--- a/solution.py
+++ b/solution.py
@@ -28,7 +28,7 @@
     flags, sinks, docs, q_hbm, k_hbm, v_hbm, g_hbm,
     out_hbm, dq_hbm, dk_hbm, dv_hbm,
     kv, qv, gv, qp, gp, ov, dqv, dkv, dkv_t,
-    kk, vv, bias, mask, hmask, scores, probs, probs_b, ds_b,
+    kk, vv, bias, mask, hmask, scores, dprobs, probs_b, ds_b,
     kv_send, kv_in, kv_diag, tail_in, fl_send, fl_in,
     qg_send, qg_in, hg_send, hg_in, og_send, og_in, dkv_send, dkv_in,
     load_sem, qload_sem, gload_sem, store_sem, sem_kv, sem_diag, sem_tail, sem_fl,
@@ -190,51 +190,68 @@
                 gp[c, a * WINDOW : (a + 1) * WINDOW, :] = merged(
                     mask, c * WINDOW, WINDOW, qg_in[i, :, there], gv[i, mine, lanes]
                 )
-        for c in range(chunks):
-            q_c, g_c, k_c, v_c = qp[c], gp[c], kk[i, c], vv[i, c]
-            scores[...] = mm(q_c, k_c, NT)
+        def products(c):
+            scores[c] = mm(qp[c], kk[i, c], NT)
+            dprobs[c] = mm(gp[c], vv[i, c], NT)
+
+        def softmax(c):
             for a in range(pairs):
                 for parity in range(2):
                     at_r = slice(a * WINDOW, (a + 1) * WINDOW)
                     at_c = slice(parity * 2 * WINDOW, (parity + 1) * 2 * WINDOW)
                     sink = sinks[i * (2 * pairs) + 2 * a + parity]
-                    s = scores[at_r, at_c] + bias[c]
+                    s = scores[c, at_r, at_c] + bias[c]
                     top = jnp.maximum(jnp.max(s, axis=1, keepdims=True), sink)
                     e = jnp.exp(s - top)
                     total = jnp.exp(sink - top) + jnp.sum(e, axis=1, keepdims=True)
-                    p = e * (1.0 / total)
-                    probs[at_r, at_c] = p
-                    probs_b[at_r, at_c] = p.astype(BF16)
-            p_c = probs_b[...]
-            out = mm(p_c, v_c, NN).astype(BF16)
-            product = g_c.astype(F32) * out.astype(F32)
+                    probs_b[c, at_r, at_c] = (e * (1.0 / total)).astype(BF16)
+
+        def outputs(c):
+            mine = slice(c * WINDOW, (c + 1) * WINDOW)
+            out = mm(probs_b[c], vv[i, c], NN).astype(BF16)
+            product = gp[c].astype(F32) * out.astype(F32)
             even = jnp.sum(jnp.where(low, product, 0.0), axis=1, keepdims=True)
             odd = jnp.sum(jnp.where(low, 0.0, product), axis=1, keepdims=True)
-            scores[...] = mm(g_c, v_c, NT)
-            for parity, dot in ((0, even), (1, odd)):
-                at_c = slice(parity * 2 * WINDOW, (parity + 1) * 2 * WINDOW)
-                ds_b[:, at_c] = (probs[:, at_c] * (scores[:, at_c] - dot)).astype(BF16)
-            ds = ds_b[...]
-            dq = mm(ds, k_c, NN).astype(BF16)
+            for a in range(pairs):
+                at_r = slice(a * WINDOW, (a + 1) * WINDOW)
+                ov[i, mine, a * 128 : (a + 1) * 128] = out[at_r]
+                for parity, dot in ((0, even), (1, odd)):
+                    at_c = slice(parity * 2 * WINDOW, (parity + 1) * 2 * WINDOW)
+                    p = probs_b[c, at_r, at_c].astype(F32)
+                    ds_b[c, at_r, at_c] = (p * (dprobs[c, at_r, at_c] - dot[at_r])).astype(BF16)
+
+        def gradients(c):
             mine = slice(c * WINDOW, (c + 1) * WINDOW)
+            ds = ds_b[c]
+            dq = mm(ds, kk[i, c], NN).astype(BF16)
             for a in range(pairs):
-                lanes = slice(a * 128, (a + 1) * 128)
-                ov[i, mine, lanes] = out[a * WINDOW : (a + 1) * WINDOW]
-                dqv[i, mine, lanes] = dq[a * WINDOW : (a + 1) * WINDOW]
-            dkt = mm(q_c, ds, TN) * scale
-            dvt = mm(g_c, p_c, TN)
+                dqv[i, mine, a * 128 : (a + 1) * 128] = dq[a * WINDOW : (a + 1) * WINDOW]
+            dkt = mm(qp[c], ds, TN) * scale
+            dvt = mm(gp[c], probs_b[c], TN)
             dkt = dkt[:half, : 2 * WINDOW] + dkt[half:, 2 * WINDOW :]
             dvt = dvt[:half, : 2 * WINDOW] + dvt[half:, 2 * WINDOW :]
             if c == 0:
                 hg_send[i, :half, :] = dkt[:, :WINDOW]
                 hg_send[i, half:, :] = dvt[:, :WINDOW]
-                hg_copy(i).start()
             else:
                 old = slice((c - 1) * WINDOW, c * WINDOW)
                 dkv_t[i, :half, old] = dkv_t[i, :half, old] + dkt[:, :WINDOW]
                 dkv_t[i, half:, old] = dkv_t[i, half:, old] + dvt[:, :WINDOW]
             dkv_t[i, :half, mine] = dkt[:, WINDOW:]
             dkv_t[i, half:, mine] = dvt[:, WINDOW:]
+
+        for c in range(chunks):
+            products(c)
+        softmax(0)
+        outputs(0)
+        for c in range(chunks):
+            if c + 1 < chunks:
+                softmax(c + 1)
+            gradients(c)
+            if c + 1 < chunks:
+                outputs(c + 1)
+            if c == 0:
+                hg_copy(i).start()
         for a in range(pairs):
             lanes = slice(a * 128, (a + 1) * 128)
             og_send[i, :, lanes] = picked(ov, (i,), lanes)
@@ -327,7 +344,8 @@
         vm((rows, 2 * kvw), BF16), vm((groups, 2 * HEAD_SIZE, rows), F32),
         vm((groups, chunks, span, 128), BF16), vm((groups, chunks, span, 128), BF16),
         vm((chunks, WINDOW, 2 * WINDOW), F32), vm((rows, 128), BF16), vm((WINDOW, 128), BF16),
-        vm((stack, span), F32), vm((stack, span), F32), vm((stack, span), BF16), vm((stack, span), BF16),
+        vm((chunks, stack, span), F32), vm((chunks, stack, span), F32),
+        vm((chunks, stack, span), BF16), vm((chunks, stack, span), BF16),
         vm((blk, 2 * kvw), BF16), vm((blk, 2 * kvw), BF16), vm((blk, 2 * kvw), BF16),
         vm((WINDOW, 2 * kvw), BF16), vm((WINDOW // blk, 128), F32), vm((WINDOW // blk, 128), F32),
         vm((groups, blk, 2 * width), BF16), vm((groups, blk, 2 * width), BF16),
@@ -349,7 +367,7 @@
         out_specs=(hbm, hbm, hbm, hbm),
         scratch_shapes=scratch,
         compiler_params=pltpu.CompilerParams(
-            collective_id=0, has_side_effects=True, vmem_limit_bytes=48 * 1024 * 1024
+            collective_id=0, has_side_effects=True, vmem_limit_bytes=65400 * 1024
         ),
         cost_estimate=pl.CostEstimate(
             flops=10 * rows * full * 2 * WINDOW, bytes_accessed=8 * rows * full, transcendentals=0

time: 37.1 us -> 33.9 us (0.914)
  local copies, waits for them, and re-layouts: 8.18 us -> 5.02 us
    unnamed x18 -> x10, local copies, waits for them, and re-layouts: 8.18 us -> 5.02 us
where the time goes in v2:
time: 33.9 us; the launch traced here: 33.6 us
  Pallas kernels  28 us (83%)
  local copies, waits for them, and re-layouts  5.02 us (15%)
  between operations  0.65 us (2%)
    pallas_call x1, Pallas kernels, shards(): pl.pallas_call(functools.partial(kernel, dims), out_shape=(big, big, smal...  28 us
    unnamed x10, local copies, waits for them, and re-layouts  5.02 us

profile of v2, /device:TPU:13, one launch (start us, length us, event | category | flops | bytes accessed | tf_op | source)
XLA Modules:
  0.0 33.6 jit_solution(10016963519996213993)
XLA Ops:
  0.6 28.0 %shard_map.102 = (bf16[256,2048]{1,0:T(8,128)(2,1)}, bf16[256,2048]{1,0:T(8,128)(2,1)}, bf16[256,256]{1,0:T(8,128)(2,1)}, bf16[256,256]{1,0:T(8,128)(2,1)}) custom-call(s32[16]{0:T(128)} %bitcast.17, f32[32]{0:T(128)} %sinks.1, s32[1,1024]{1,0:T(1,128)} %docs.1, bf16[256,2048]{1,0:T(8,128)(2,1)} %bitcast.13, bf16[256,256]{1,0:T(8,128)(2,1)} %bitcast.15, ...), custom_call_target="tpu_custom_call" | custom-call | flops 1342177280 | bytes 4194304 | tf_op jit(solution)/shard_map/pallas_call | solution.py:363
  28.6 0.0 copy-start
  28.6 2.4 %copy.15 = bf16[1,256,2048]{2,1,0:T(8,128)(2,1)} copy(bf16[1,256,2048]{2,1,0:T(8,128)(2,1)} %bitcast.10) | data formatting | bytes 2097152
  31.0 0.0 copy-done
  31.0 0.0 copy-start.2
  31.0 1.0 %copy.16 = bf16[1,256,2048]{2,1,0:T(8,128)(2,1)} copy(bf16[1,256,2048]{2,1,0:T(8,128)(2,1)S(1)} %bitcast.9) | data formatting | bytes 2097152
  32.0 0.1 copy-done.2
  32.0 0.0 copy-start.1
  32.0 0.7 %copy.17 = bf16[1,256,256]{2,1,0:T(8,128)(2,1)} copy(bf16[1,256,256]{2,1,0:T(8,128)(2,1)S(1)} %bitcast.12) | data formatting | bytes 262144
  32.7 0.3 copy-done.1
  33.0 0.7 %copy.18 = bf16[1,256,256]{2,1,0:T(8,128)(2,1)} copy(bf16[1,256,256]{2,1,0:T(8,128)(2,1)S(1)} %bitcast.11) | data formatting | bytes 262144
Async XLA Ops:
  28.6 2.4 %copy-start = (bf16[256,2048]{1,0:T(8,128)(2,1)S(1)}, bf16[256,2048]{1,0:T(8,128)(2,1)}, u32[]{:S(2)}) copy-start(bf16[256,2048]{1,0:T(8,128)(2,1)} %get-tuple-element.9) | copy-start | bytes 3145732
  31.0 1.0 %copy-start.2 = (bf16[256,256]{1,0:T(8,128)(2,1)S(1)}, bf16[256,256]{1,0:T(8,128)(2,1)}, u32[]{:S(2)}) copy-start(bf16[256,256]{1,0:T(8,128)(2,1)} %get-tuple-element.10) | copy-start | bytes 393220
  32.0 1.0 %copy-start.1 = (bf16[256,256]{1,0:T(8,128)(2,1)S(1)}, bf16[256,256]{1,0:T(8,128)(2,1)}, u32[]{:S(2)}) copy-start(bf16[256,256]{1,0:T(8,128)(2,1)} %get-tuple-element.11) | copy-start | bytes 393220

commit v3 on v2

--- a/solution.py
+++ b/solution.py
@@ -319,6 +319,28 @@
         dq_store(i).wait()
     dk_store.wait()
     dv_store.wait()
+
+
+def hand_over(parts, *refs):
+    count = len(parts)
+    sources, targets, held = refs[:count], refs[count : 2 * count], refs[2 * count : 3 * count]
+    load_sem, store_sem = refs[3 * count :]
+    loads, stores = [], []
+    slot = 0
+    for n, cuts in enumerate(parts):
+        size = sources[n].shape[0] // cuts
+        for cut in range(cuts):
+            at = pl.ds(cut * size, size)
+            loads.append(pltpu.make_async_copy(sources[n].at[at, :], held[n].at[at, :], load_sem.at[slot]))
+            stores.append(pltpu.make_async_copy(held[n].at[at, :], targets[n].at[at, :], store_sem.at[slot]))
+            slot += 1
+    for load in loads:
+        load.start()
+    for load, store in zip(loads, stores):
+        load.wait()
+        store.start()
+    for store in stores:
+        store.wait()
 
 
 def shards(queries, keys, values, grad_out, sinks, doc_ids, swap_flags):
@@ -373,6 +395,17 @@
             flops=10 * rows * full * 2 * WINDOW, bytes_accessed=8 * rows * full, transcendentals=0
         ),
     )(swap_flags[0, 0], sinks, doc_ids, queries[0], keys[0], values[0], grad_out[0])
+    parts = (4, 4, 1, 1)
+    shapes = (big, big, small, small)
+    results = pl.pallas_call(
+        functools.partial(hand_over, parts),
+        out_shape=shapes,
+        in_specs=[hbm] * len(parts),
+        out_specs=(hbm,) * len(parts),
+        scratch_shapes=[vm(shape.shape, BF16) for shape in shapes] + [dma((sum(parts),)), dma((sum(parts),))],
+        compiler_params=pltpu.CompilerParams(vmem_limit_bytes=65400 * 1024),
+        cost_estimate=pl.CostEstimate(flops=0, bytes_accessed=9 * rows * full, transcendentals=0),
+    )(*results)
     return tuple(result[None] for result in results)
 
 

time: 33.9 us -> 31.3 us (0.923)
  local copies, waits for them, and re-layouts: 5.02 us -> 0 us
  Pallas kernels: 28 us -> 30.5 us
    unnamed x10 -> x0, local copies, waits for them, and re-layouts: 5.02 us -> none
    pallas_call x0 -> x1, Pallas kernels: none -> 2.51 us  [shards(): pl.pallas_call(functools.partial(hand_over, parts), out_shape=shapes, in_...]
where the time goes in v3:
time: 31.3 us; the launch traced here: 31.1 us
  Pallas kernels  30.5 us (97%)
  between operations  0.64 us (2%)
    pallas_call x1, Pallas kernels, shards(): pl.pallas_call(functools.partial(kernel, dims), out_shape=(big, big, smal...  28 us
    pallas_call x1, Pallas kernels, shards(): pl.pallas_call(functools.partial(hand_over, parts), out_shape=shapes, in_...  2.51 us

profile of v3, /device:TPU:13, one launch (start us, length us, event | category | flops | bytes accessed | tf_op | source)
XLA Modules:
  0.0 31.1 jit_solution(16960267853514681308)
XLA Ops:
  0.6 28.0 %shard_map.102 = (bf16[256,2048]{1,0:T(8,128)(2,1)}, bf16[256,2048]{1,0:T(8,128)(2,1)}, bf16[256,256]{1,0:T(8,128)(2,1)}, bf16[256,256]{1,0:T(8,128)(2,1)}) custom-call(s32[16]{0:T(128)} %bitcast.17, f32[32]{0:T(128)} %sinks.1, s32[1,1024]{1,0:T(1,128)} %docs.1, bf16[256,2048]{1,0:T(8,128)(2,1)} %bitcast.9, bf16[256,256]{1,0:T(8,128)(2,1)} %bitcast.13, ...), custom_call_target="tpu_custom_call" | custom-call | flops 1342177280 | bytes 4194304 | tf_op jit(solution)/shard_map/pallas_call | solution.py:385
  28.6 2.5 %shard_map.103 = (bf16[256,2048]{1,0:T(8,128)(2,1)}, bf16[256,2048]{1,0:T(8,128)(2,1)}, bf16[256,256]{1,0:T(8,128)(2,1)}, bf16[256,256]{1,0:T(8,128)(2,1)}) custom-call(bf16[256,2048]{1,0:T(8,128)(2,1)} %get-tuple-element.12.refs_0_, bf16[256,2048]{1,0:T(8,128)(2,1)} %get-tuple-element.13.refs_1_, bf16[256,256]{1,0:T(8,128)(2,1)} %get-tuple-element.14.refs_2_, ...), custom_call_target="tpu_custom_call" | custom-call | bytes 4718592 | tf_op jit(solution)/shard_map/pallas_call | solution.py:400

commit v4 on v3

--- a/solution.py
+++ b/solution.py
@@ -259,7 +259,7 @@
         og_copy(i).start()
         return carry
 
-    lax.fori_loop(0, groups, group_step, 0)
+    lax.fori_loop(0, groups, group_step, 0, unroll=2)
 
     for i in range(groups):
         hg_copy(i).wait_recv()

time: 31.3 us -> 31.4 us (level)
  no operation moved by 1% of the time
where the time goes in v4:
time: 31.4 us; the launch traced here: 31.1 us
  Pallas kernels  30.5 us (97%)
  between operations  0.64 us (2%)
    pallas_call x1, Pallas kernels, shards(): pl.pallas_call(functools.partial(kernel, dims), out_shape=(big, big, smal...  28 us
    pallas_call x1, Pallas kernels, shards(): pl.pallas_call(functools.partial(hand_over, parts), out_shape=shapes, in_...  2.51 us

profile of v4, /device:TPU:13, one launch (start us, length us, event | category | flops | bytes accessed | tf_op | source)
XLA Modules:
  0.0 31.1 jit_solution(16312408871586713390)
XLA Ops:
  0.6 28.0 %shard_map.102 = (bf16[256,2048]{1,0:T(8,128)(2,1)}, bf16[256,2048]{1,0:T(8,128)(2,1)}, bf16[256,256]{1,0:T(8,128)(2,1)}, bf16[256,256]{1,0:T(8,128)(2,1)}) custom-call(s32[16]{0:T(128)} %bitcast.17, f32[32]{0:T(128)} %sinks.1, s32[1,1024]{1,0:T(1,128)} %docs.1, bf16[256,2048]{1,0:T(8,128)(2,1)} %bitcast.9, bf16[256,256]{1,0:T(8,128)(2,1)} %bitcast.13, ...), custom_call_target="tpu_custom_call" | custom-call | flops 1342177280 | bytes 4194304 | tf_op jit(solution)/shard_map/pallas_call | solution.py:385
  28.6 2.5 %shard_map.103 = (bf16[256,2048]{1,0:T(8,128)(2,1)}, bf16[256,2048]{1,0:T(8,128)(2,1)}, bf16[256,256]{1,0:T(8,128)(2,1)}, bf16[256,256]{1,0:T(8,128)(2,1)}) custom-call(bf16[256,2048]{1,0:T(8,128)(2,1)} %get-tuple-element.12.refs_0_, bf16[256,2048]{1,0:T(8,128)(2,1)} %get-tuple-element.13.refs_1_, bf16[256,256]{1,0:T(8,128)(2,1)} %get-tuple-element.14.refs_2_, ...), custom_call_target="tpu_custom_call" | custom-call | bytes 4718592 | tf_op jit(solution)/shard_map/pallas_call | solution.py:400
